TPU v7x, 32 devices: a whole 2x2x4 slice. The times are simulated.
32 devices in a mesh: grp: 8 (over y, x, core), tp: 4 (over z).
Axes of the slice: x: 2, y: 2, z: 4, core: 2. Of those that a mesh axis runs over, the one named last changes fastest.
Arguments:
- queries: bfloat16 [32, 2, 4096], P('grp'), may hold values from -8 to 8
- cache_keys: bfloat16 [32, 512, 512], P('grp', 'tp'), may hold values from -8 to 8
- cache_values: bfloat16 [32, 512, 512], P('grp', 'tp'), may hold values from -6 to 6
- new_keys: bfloat16 [32, 2, 512], P('grp'), may hold values from -6 to 6
- new_values: bfloat16 [32, 2, 512], P('grp'), may hold values from -6 to 6
- lengths: int32 [32], P('grp'), may hold values from 2 to 512
- residual: bfloat16 [32, 2, 4096], P('grp'), may hold values from -0.1796875 to 0.1796875
- norm_gain: float32 [4096], replicated, may hold values from 0.25 to 1.75
- w_gate: float32 [4096, 2400], P('grp', 'tp'), may hold values from -0.09375 to 0.09375
- w_down: float32 [4096, 2400], P('grp', 'tp'), may hold values from -0.125 to 0.125
Outputs:
- mixed: bfloat16 [32, 2, 4096], P('grp')
All inputs are finite; a program needn't handle non-finite values.
Results may differ from a plain program's by a relative error of at most 0.028.
Values may be sent and summed in bfloat16 or wider, within the bound.
A program may use at most 64 MiB of HBM per device.

v0:
```python
import functools

import jax
import jax.numpy as jnp
from jax import lax
from jax.experimental import pallas as pl
from jax.experimental.pallas import tpu as pltpu
from jax.sharding import PartitionSpec as P

HD = 128
KVH = 4


masked_score = -1e30


def merged_2(shard, axis, join):
    gathered = jax.tree.map(
        lambda a, kind: lax.all_gather(a.astype(kind), axis),
        shard,
        jax.tree.map(lambda a: jnp.bfloat16 if a.dtype == jnp.float32 else a.dtype, shard),
    )

    def take(source):
        return jax.tree.map(
            lambda a, own: lax.dynamic_index_in_dim(a, source, 0, False).astype(own.dtype),
            gathered,
            shard,
        )

    return lax.fori_loop(
        1, lax.axis_size(axis), lambda source, state: join(state, take(source)), take(0)
    )


def combine_parts(earlier, later):
    first_max, first_total, first_accum = earlier
    second_max, second_total, second_accum = later
    joint_max = jnp.maximum(first_max, second_max)
    first_factor = jnp.exp(first_max - joint_max)
    second_factor = jnp.exp(second_max - joint_max)
    joint_total = first_total * first_factor + second_total * second_factor
    joint_accum = first_accum * first_factor[..., None] + second_accum * second_factor[..., None]
    return (joint_max, joint_total, joint_accum)


def partial_softmax(scores, visible, value_heads, formula):
    scores = jnp.where(visible, scores, masked_score)
    highest = jnp.max(scores, axis=-1)
    weights = jnp.where(visible, jnp.exp(scores - highest[..., None]), 0.0)
    totals = jnp.sum(weights, axis=-1)
    accum = jnp.einsum(
        formula, weights.astype(jnp.bfloat16), value_heads, preferred_element_type=jnp.float32
    )
    return (highest, totals, accum)


def gathered_weights(
    queries,
    cache_keys,
    cache_values,
    new_keys,
    new_values,
    lengths,
    residual,
    norm_gain,
    w_gate,
    w_down,
):
    row_count, step_count, features = queries.shape
    positions = cache_keys.shape[1]
    per_group = features // (KVH * HD)
    inv_root = HD ** (-0.5)
    query_heads = queries.reshape(row_count, step_count, KVH, per_group, HD)
    key_heads = cache_keys.reshape(row_count, positions, KVH, HD)
    value_heads = cache_values.reshape(row_count, positions, KVH, HD)
    cached_scores = (
        jnp.einsum("rsjgd,rcjd->rsjgc", query_heads, key_heads, preferred_element_type=jnp.float32)
        * inv_root
    )
    offset = lax.axis_index("tp") * positions
    places = offset + lax.broadcasted_iota(jnp.int32, (row_count, positions), 1)
    visible = (places < lengths[:, None])[:, None, None, None, :]
    local_part = partial_softmax(cached_scores, visible, value_heads, "rsjgc,rcjd->rsjgd")
    merged = merged_2(local_part, "tp", combine_parts)
    fresh_key_heads = new_keys.reshape(row_count, step_count, KVH, HD)
    fresh_value_heads = new_values.reshape(row_count, step_count, KVH, HD)
    fresh_scores = (
        jnp.einsum(
            "rsjgd,rtjd->rsjgt", query_heads, fresh_key_heads, preferred_element_type=jnp.float32
        )
        * inv_root
    )
    causal = lax.broadcasted_iota(jnp.int32, (step_count, step_count), 0) >= lax.broadcasted_iota(
        jnp.int32, (step_count, step_count), 1
    )
    causal = causal[None, :, None, None, :]
    fresh_part = partial_softmax(fresh_scores, causal, fresh_value_heads, "rsjgt,rtjd->rsjgd")
    joint_max, joint_total, joint_accum = combine_parts(merged, fresh_part)
    context = (joint_accum / joint_total[..., None]).reshape(row_count, step_count, features)
    summed = residual.astype(jnp.float32) + context
    mean_square = jnp.mean(summed * summed, axis=-1, keepdims=True)
    normed = (summed * lax.rsqrt(mean_square + 1e-05) * norm_gain).astype(jnp.bfloat16)
    flat = normed.reshape(row_count * step_count, features)
    gate_policy, down_policy = (
        lax.all_gather(w_gate.astype(jnp.bfloat16), "grp", axis=0, tiled=True),
        lax.all_gather(w_down.astype(jnp.bfloat16), "grp", axis=0, tiled=True),
    )
    gate = jnp.dot(flat, gate_policy, preferred_element_type=jnp.float32)
    hidden = jax.nn.silu(gate).astype(jnp.bfloat16)
    partial_sum = lax.dot_general(
        hidden, down_policy, (((1,), (1,)), ((), ())), preferred_element_type=jnp.float32
    )
    mlp = lax.psum(partial_sum.astype(jnp.bfloat16), "tp").astype(jnp.float32)
    return (summed + mlp.reshape(row_count, step_count, features)).astype(jnp.bfloat16)


MESH = pl.DeviceIdType.MESH
BF16, F32 = jnp.bfloat16, jnp.float32


def layer_kernel(
    n_g,
    n_t,
    lengths_hbm,
    q_hbm,
    nk_hbm,
    nv_hbm,
    res_hbm,
    gain_hbm,
    ck_hbm,
    cv_hbm,
    wg_hbm,
    wd_hbm,
    out_ref,
    lengths_ref,
    q_in,
    nk_in,
    nv_in,
    res_in,
    gain,
    ck,
    cv,
    wg32,
    wd32,
    wg,
    wd,
    q_rows,
    res_rows,
    nk_rows,
    nv_rows,
    send_o,
    recv_o,
    send_x,
    recv_x,
    x_rows,
    x_flat,
    send_g,
    recv_g,
    send_h,
    recv_h,
    send_m,
    recv_m,
    send_f,
    load_sem,
    o_send_sem,
    o_recv_sem,
    m_send_sem,
    m_recv_sem,
    g_send_sem,
    g_recv_sem,
    h_send_sem,
    h_recv_sem,
    x_send_sem,
    x_recv_sem,
    f_send_sem,
    f_recv_sem,
):
    g, t = lax.axis_index("grp"), lax.axis_index("tp")
    rows, positions = ck.shape[0], ck.shape[1]
    steps = nk_in.shape[1]
    heads = gain.shape[0]
    units, depth = wg32.shape
    per_key = heads // KVH
    per_col = heads // n_g
    halves = per_key // per_col
    height = steps * per_col
    inv_root = HD ** (-0.5)
    group_rows = rows * steps
    half_t = n_t // 2

    peer_g = [g] + [lax.rem(g + k, n_g) for k in range(1, n_g)]
    peer_t = [t] + [lax.rem(t + k, n_t) for k in range(1, n_t)]
    far_first = sorted(range(n_t), key=lambda k: (k == 0, abs(k - half_t)))

    barrier = pltpu.get_barrier_semaphore()
    for peer in [(i, t) for i in peer_g[1:]] + [(g, k) for k in peer_t[1:]]:
        pl.semaphore_signal(barrier, inc=1, device_id=peer, device_id_type=MESH)

    loads = [
        pltpu.make_async_copy(source, target, load_sem.at[i])
        for i, (source, target) in enumerate(
            (
                (q_hbm, q_in),
                (lengths_hbm, lengths_ref),
                (ck_hbm, ck),
                (cv_hbm, cv),
                (nk_hbm, nk_in),
                (nv_hbm, nv_in),
                (res_hbm, res_in),
                (gain_hbm, gain),
                (wg_hbm, wg32),
                (wd_hbm, wd32),
            )
        )
    ]
    for load in loads:
        load.start()

    def blocks_of(at):
        first = (at % 2) * n_t + at // 2
        return first, first + half_t

    mine = (lax.rem(t, 2) * n_t + t // 2, lax.rem(t, 2) * n_t + t // 2 + half_t)

    def by_block(source, target):
        flat = jnp.concatenate([source[r].astype(F32) for r in range(rows)], axis=0)
        for h in range(heads):
            target[h // per_col, pl.ds(h % per_col, group_rows, stride=per_col), :] = flat[
                :, h * HD : (h + 1) * HD
            ]

    loads[0].wait()
    by_block(q_in, q_rows)
    loads[1].wait()
    loads[2].wait()
    lane_place = t * positions + lax.broadcasted_iota(jnp.int32, (halves * height, positions), 1)
    pieces, shown = [], []
    tall = halves * height
    blank = jnp.zeros((tall, HD), F32)
    for r in range(rows):
        visible = (lane_place < lengths_ref[r]).astype(F32)
        query = []
        for j in range(KVH):
            own = jnp.concatenate(
                [
                    q_rows[j * halves + i, r * height : (r + 1) * height]
                    for i in range(halves)
                ],
                axis=0,
            )
            query.append(jnp.concatenate([blank] * j + [own] + [blank] * (KVH - 1 - j), axis=1))
            shown.append(visible)
        pieces.append(
            lax.dot_general(
                jnp.concatenate(query, axis=0).astype(BF16),
                ck[r],
                (((1,), (1,)), ((), ())),
                preferred_element_type=F32,
            )
        )
    shown = jnp.concatenate(shown, axis=0) > 0.0
    scores = jnp.where(shown, jnp.concatenate(pieces, axis=0) * inv_root, masked_score)
    highest = jnp.max(scores, axis=-1, keepdims=True)
    weights = jnp.where(shown, jnp.exp(scores - highest), 0.0)
    total = jnp.sum(weights, axis=-1, keepdims=True)
    weights = weights.astype(BF16)
    loads[3].wait()
    accum = []
    for r in range(rows):
        wide = jnp.dot(
            weights[r * KVH * tall : (r + 1) * KVH * tall], cv[r], preferred_element_type=F32
        )
        for j in range(KVH):
            accum.append(wide[j * tall : (j + 1) * tall, j * HD : (j + 1) * HD])
    some = total > 0.0
    safe = jnp.where(some, total, 1.0)
    means = jnp.concatenate(accum, axis=0) / safe
    logs = jnp.where(some, highest + jnp.log(safe), masked_score)

    def of_owner(array, at, i):
        b = blocks_of(at)[i]
        starts = [
            (r * KVH + b // halves) * tall + (b % halves) * height for r in range(rows)
        ]
        return jnp.concatenate([array[at : at + height] for at in starts], axis=0)

    block_rows = rows * height
    diagonal = lax.broadcasted_iota(jnp.int32, (block_rows, HD), 0) == lax.broadcasted_iota(
        jnp.int32, (block_rows, HD), 1
    )
    place = lax.broadcasted_iota(jnp.int32, (send_o.shape[2] - block_rows, HD), 0)

    def fill(at, i):
        lanes = jnp.sum(jnp.where(diagonal, of_owner(logs, at, i), 0.0), axis=0, keepdims=True)
        high = lanes.astype(BF16).astype(F32)
        middle = (lanes - high).astype(BF16).astype(F32)
        low = lanes - high - middle
        terms = jnp.where(place == 0, high, jnp.where(place == 1, middle, low))
        send_o[i, at] = jnp.concatenate([of_owner(means, at, i), terms], axis=0).astype(BF16)

    def along_tp(k, i, source, target, send_sem, recv_sem):
        return pltpu.make_async_remote_copy(
            src_ref=source.at[i, peer_t[k]],
            dst_ref=target.at[i, t],
            send_sem=send_sem.at[i * n_t + k],
            recv_sem=recv_sem.at[i * n_t + k],
            device_id=(g, peer_t[k]),
            device_id_type=MESH,
        )

    for i in range(2):
        for at in range(n_t):
            fill(at, i)
    pl.semaphore_wait(barrier, n_g + n_t - 2)
    row_copies = [
        [along_tp(k, i, send_o, recv_o, o_send_sem, o_recv_sem) for k in far_first[:-1]]
        for i in range(2)
    ]
    for i in range(2):
        for copy in row_copies[i]:
            copy.start()
        recv_o[i, t] = send_o[i, t]

    for load in loads[4:8]:
        load.wait()
    by_block(res_in, res_rows)
    for source, target in ((nk_in, nk_rows), (nv_in, nv_rows)):
        flat = jnp.concatenate([source[r].astype(F32) for r in range(rows)], axis=0)
        for j in range(KVH):
            target[j] = flat[:, j * HD : (j + 1) * HD]

    def new_tokens(tokens, at, b):
        held = tokens[b // halves]
        return jnp.concatenate(
            [
                jnp.broadcast_to(held[r * steps + at : r * steps + at + 1], (height, HD))
                for r in range(rows)
            ],
            axis=0,
        )

    step_of = lax.broadcasted_iota(jnp.int32, (block_rows, 1), 0) & (height - 1)
    seen = [step_of >= at * per_col for at in range(steps)]
    fresh = [
        [
            jnp.where(
                seen[at],
                jnp.sum(q_rows[b] * new_tokens(nk_rows, at, b), axis=-1, keepdims=True)
                * inv_root,
                masked_score,
            )
            for at in range(steps)
        ]
        for b in mine
    ]
    new_held = [[new_tokens(nv_rows, at, b) for at in range(steps)] for b in mine]
    loads[8].wait()
    spare = jnp.zeros((wg.shape[0] - units, depth), F32)
    wg[...] = jnp.concatenate([wg32[...], spare], axis=0).astype(BF16)

    def finish_context(i):
        logs = []
        for at in range(n_t):
            terms = recv_o[i, at, block_rows:].astype(F32)
            lanes = terms[0:1] + terms[1:2] + terms[2:3]
            logs.append(jnp.sum(jnp.where(diagonal, lanes, 0.0), axis=-1, keepdims=True))
        joint = functools.reduce(jnp.maximum, logs + fresh[i])
        total, accum = 0.0, 0.0
        for at in range(n_t):
            weight = jnp.exp(logs[at] - joint)
            total = total + weight
            accum = accum + weight * recv_o[i, at, :block_rows].astype(F32)
        for at in range(steps):
            weight = jnp.where(seen[at], jnp.exp(fresh[i][at] - joint), 0.0)
            total = total + weight
            accum = accum + weight.astype(BF16).astype(F32) * new_held[i][at]
        send_x[i] = (res_rows[mine[i]] + accum / total).astype(BF16)

    class Spread:
        def __init__(self, source, target, send_sem, recv_sem):
            self.refs = source, target, send_sem, recv_sem

        def each(self, action, parts):
            source, target, send_sem, recv_sem = self.refs
            for i in parts:
                for k in far_first:
                    copy = pltpu.make_async_remote_copy(
                        src_ref=source.at[i],
                        dst_ref=target(g),
                        send_sem=send_sem.at[i * n_t + k],
                        recv_sem=recv_sem.at[g],
                        device_id=(mine[i], peer_t[k]),
                        device_id_type=MESH,
                    )
                    if k:
                        action(copy)
                    else:
                        pl.when(mine[i] != g)(functools.partial(action, copy))

        def start(self, i):
            self.each(lambda copy: copy.start(), (i,))
            source, target, _, recv_sem = self.refs
            here = pltpu.make_async_copy(source.at[i], target(g), recv_sem.at[g])
            pl.when(mine[i] == g)(here.start)

        def wait_send(self):
            self.each(lambda copy: copy.wait_send(), range(2))

        def wait_recv(self, parts):
            source, target, _, recv_sem = self.refs
            for i in parts:
                pltpu.make_async_copy(source.at[0], target(i), recv_sem.at[i]).wait()

    x_spread = Spread(send_x, lambda i: recv_x.at[i], x_send_sem, x_recv_sem)
    for i in range(2):
        for copy in row_copies[i]:
            copy.wait_recv()
        finish_context(i)
        x_spread.start(i)

    parts = [[blocks_of(at)[i] for at in range(n_t)] for i in range(2)]
    part_rows = n_t * group_rows
    gains = [gain[pl.ds(g * per_col + c, 1)] for c in range(per_col)]

    def part_gate(i):
        x_spread.wait_recv(parts[i])
        x_rows[i] = jnp.concatenate([recv_x[b].astype(F32) for b in parts[i]], axis=0)
        columns = [
            x_rows.at[i][pl.ds(c, part_rows, stride=per_col), :] for c in range(per_col)
        ]
        squares = jnp.sum(
            functools.reduce(jnp.add, [c * c for c in columns]), axis=-1, keepdims=True
        )
        scaled = jnp.concatenate([c * by for c, by in zip(columns, gains)], axis=1).astype(BF16)
        gate = lax.dot_general(
            scaled, wg[...], (((1,), (1,)), ((), ())), preferred_element_type=F32
        )
        spare_lane = lax.broadcasted_iota(jnp.int32, gate.shape, 1) >= units
        gate = jnp.where(spare_lane, squares, gate)
        for at, b in enumerate(parts[i]):
            send_g[b] = gate[at * group_rows : (at + 1) * group_rows].astype(BF16)
        return columns

    def along_grp(k, source, target, send_sem, recv_sem):
        return pltpu.make_async_remote_copy(
            src_ref=source,
            dst_ref=target.at[g],
            send_sem=send_sem.at[k - 1],
            recv_sem=recv_sem.at[k - 1],
            device_id=(peer_g[k], t),
            device_id_type=MESH,
        )

    gate_copies = [
        along_grp(k, send_g.at[peer_g[k]], recv_g, g_send_sem, g_recv_sem) for k in range(1, n_g)
    ]
    for i in range(2):
        columns = part_gate(i)
        for k in range(1, n_g):
            in_part = functools.reduce(jnp.logical_or, [peer_g[k] == b for b in parts[i]])
            pl.when(in_part)(gate_copies[k - 1].start)
        wide = jnp.concatenate(columns, axis=1)
        for at, b in enumerate(parts[i]):
            x_flat[b] = wide[at * group_rows : (at + 1) * group_rows]
    recv_g[g] = send_g[g]
    loads[9].wait()
    wd[...] = jnp.concatenate([wd32[...], spare], axis=0).astype(BF16)
    for copy in gate_copies:
        copy.wait_recv()
    whole = functools.reduce(jnp.add, [recv_g[i].astype(F32) for i in range(n_g)])
    square = whole[:, units : units + 1]
    whole = whole * lax.rsqrt(square / (heads * HD) + 1e-05)
    own_hidden = (whole / (1.0 + jnp.exp(-whole))).astype(BF16)

    send_h[...] = own_hidden
    hidden_copies = [
        pltpu.make_async_remote_copy(
            src_ref=send_h,
            dst_ref=recv_h.at[g],
            send_sem=h_send_sem.at[k],
            recv_sem=h_recv_sem.at[g],
            device_id=(peer_g[k], t),
            device_id_type=MESH,
        )
        for k in range(1, n_g)
    ]
    for copy in hidden_copies:
        copy.start()
    pltpu.make_async_copy(send_h, recv_h.at[g], h_recv_sem.at[g]).start()

    mlp_copies = [
        [along_tp(k, i, send_m, recv_m, m_send_sem, m_recv_sem) for k in far_first[:-1]]
        for i in range(2)
    ]
    for i in range(2):
        for b in parts[i]:
            pltpu.make_async_copy(send_h, recv_h.at[b], h_recv_sem.at[b]).wait()
        hidden = jnp.concatenate([recv_h[b].astype(F32) for b in parts[i]], axis=0).astype(BF16)
        mlp = jnp.dot(hidden, wd[...], preferred_element_type=F32)
        for at in range(n_t):
            send_m[i, at] = mlp[at * group_rows : (at + 1) * group_rows].astype(BF16)
        for copy in mlp_copies[i]:
            copy.start()
        recv_m[i, t] = send_m[i, t]

    def out_columns(i):
        return out_ref.at[:, :, pl.ds(pl.multiple_of(i * depth, depth), depth)]

    f_spread = Spread(send_f, out_columns, f_send_sem, f_recv_sem)
    for i in range(2):
        for copy in mlp_copies[i]:
            copy.wait_recv()
        done = functools.reduce(jnp.add, [recv_m[i, at].astype(F32) for at in range(n_t)])
        done = (x_flat[mine[i]] + done).astype(BF16)
        for r in range(rows):
            send_f[i, r] = done[r * steps : (r + 1) * steps]
        f_spread.start(i)
    for copy in row_copies[0] + row_copies[1] + gate_copies + hidden_copies:
        copy.wait_send()
    for copy in mlp_copies[0] + mlp_copies[1]:
        copy.wait_send()
    x_spread.wait_send()
    f_spread.wait_recv(range(n_g))
    f_spread.wait_send()


def moved_activations(
    n_g,
    n_t,
    queries,
    cache_keys,
    cache_values,
    new_keys,
    new_values,
    lengths,
    residual,
    norm_gain,
    w_gate,
    w_down,
):
    rows, steps, features = queries.shape
    positions, kv_width = cache_keys.shape[1:]
    depth, units = w_gate.shape
    heads = features // HD
    per_col = heads // n_g
    height = steps * per_col
    group_rows = rows * steps
    wide = (units // HD + 1) * HD
    hbm = pl.BlockSpec(memory_space=pltpu.HBM)
    dma = pltpu.SemaphoreType.DMA
    return pl.pallas_call(
        functools.partial(layer_kernel, n_g, n_t),
        out_shape=pltpu.VMEM(queries.shape, BF16),
        in_specs=[hbm] * 10,
        out_specs=pl.BlockSpec(memory_space=pltpu.VMEM),
        scratch_shapes=[
            pltpu.SMEM(lengths.shape, jnp.int32),
            pltpu.VMEM(queries.shape, BF16),
            pltpu.VMEM(new_keys.shape, BF16),
            pltpu.VMEM(new_values.shape, BF16),
            pltpu.VMEM(residual.shape, BF16),
            pltpu.VMEM((heads, HD), F32),
            pltpu.VMEM(cache_keys.shape, BF16),
            pltpu.VMEM(cache_values.shape, BF16),
            pltpu.VMEM((units, depth), F32),
            pltpu.VMEM((units, depth), F32),
            pltpu.VMEM((wide, depth), BF16),
            pltpu.VMEM((wide, depth), BF16),
            pltpu.VMEM((n_g, rows * height, HD), F32),
            pltpu.VMEM((n_g, rows * height, HD), F32),
            pltpu.VMEM((KVH, group_rows, HD), F32),
            pltpu.VMEM((KVH, group_rows, HD), F32),
            pltpu.VMEM((2, n_t, rows * height + 16, HD), BF16),
            pltpu.VMEM((2, n_t, rows * height + 16, HD), BF16),
            pltpu.VMEM((2, rows * height, HD), BF16),
            pltpu.VMEM((n_g, rows * height, HD), BF16),
            pltpu.VMEM((2, n_t * rows * height, HD), F32),
            pltpu.VMEM((n_g, group_rows, depth), F32),
            pltpu.VMEM((n_g, group_rows, wide), BF16),
            pltpu.VMEM((n_g, group_rows, wide), BF16),
            pltpu.VMEM((group_rows, wide), BF16),
            pltpu.VMEM((n_g, group_rows, wide), BF16),
            pltpu.VMEM((2, n_t, group_rows, depth), BF16),
            pltpu.VMEM((2, n_t, group_rows, depth), BF16),
            pltpu.VMEM((2, rows, steps, depth), BF16),
            dma((10,)),
        ]
        + [dma((2 * n_t,))] * 4
        + [dma((n_g,))] * 8,
        compiler_params=pltpu.CompilerParams(
            collective_id=0, has_side_effects=True, vmem_limit_bytes=40 * 1024 * 1024
        ),
    )(
        *(
            pltpu.with_memory_space_constraint(array, pltpu.HBM)
            for array in (
                lengths,
                queries,
                new_keys,
                new_values,
                residual,
                norm_gain.reshape(heads, HD),
                cache_keys,
                cache_values,
                w_gate.T,
                w_down.T,
            )
        ),
    )


def shards(n_g, n_t, *arrays):
    queries, cache_keys = arrays[0], arrays[1]
    rows, steps, features = queries.shape
    heads = features // HD
    kv_heads = cache_keys.shape[2] // HD
    even = (
        n_g == 2 * n_t
        and n_t % 2 == 0
        and heads % n_g == 0
        and n_g % kv_heads == 0
        and steps * (heads // n_g) == 8
        and rows * steps == 8
    )
    if even:
        return moved_activations(n_g, n_t, *arrays)
    return gathered_weights(*arrays)


def solution(mesh):
    return jax.shard_map(
        functools.partial(shards, mesh.shape["grp"], mesh.shape["tp"]),
        mesh=mesh,
        in_specs=(
            P("grp", None, None),
            P("grp", "tp", None),
            P("grp", "tp", None),
            P("grp", None, None),
            P("grp", None, None),
            P("grp"),
            P("grp", None, None),
            P(),
            P("grp", "tp"),
            P("grp", "tp"),
        ),
        out_specs=P("grp", None, None),
        check_vma=False,
    )
```

profile of v0, /device:TPU:0, one launch (start us, length us, event | category | flops | bytes accessed | tf_op | source)
XLA Modules:
  0.0 29.6 jit_solution(17598885009019372463)
XLA Ops:
  0.0 28.9 %shard_map.100 = bf16[4,2,4096]{2,1,0:T(2,128)(2,1)S(1)} custom-call(s32[4]{0:T(128)} %lengths_hbm.1, bf16[4,2,4096]{2,1,0:T(2,128)(2,1)} %q_hbm.1, bf16[4,2,512]{2,1,0:T(2,128)(2,1)} %nk_hbm.1, bf16[4,2,512]{2,1,0:T(2,128)(2,1)} %nv_hbm.1, bf16[4,2,4096]{2,1,0:T(2,128)(2,1)} %res_hbm.1, f32[32,128]{1,0:T(8,128)} %bitcast.5, bf16[4,128,512]{2,1,0:T(8,128)(2,1)} %ck_hbm.1, ...), custom_call_target="tpu_custom_call" | custom-call | tf_op jit(solution)/shard_map/pallas_call | solution.py:552
  28.9 0.6 %copy.12 = bf16[4,2,4096]{2,1,0:T(2,128)(2,1)} copy(bf16[4,2,4096]{2,1,0:T(2,128)(2,1)S(1)} %shard_map.100) | data formatting | bytes 131072
where the time goes:
time: 29.7 us; the launch traced here: 29.6 us
  Pallas kernels  28.9 us (97%)
  local copies, waits for them, and re-layouts  0.63 us (2%)
    pallas_call x1, Pallas kernels, moved_activations(): pl.pallas_call(functools.partial(layer_kernel, n_g, n_t), out_shape=pltpu...  28.9 us
    unnamed x1, local copies, waits for them, and re-layouts  0.63 us

commit v1 on v0

--- a/solution.py
+++ b/solution.py
@@ -286,18 +286,37 @@
         return jnp.concatenate([array[at : at + height] for at in starts], axis=0)
 
     block_rows = rows * height
-    diagonal = lax.broadcasted_iota(jnp.int32, (block_rows, HD), 0) == lax.broadcasted_iota(
-        jnp.int32, (block_rows, HD), 1
-    )
-    place = lax.broadcasted_iota(jnp.int32, (send_o.shape[2] - block_rows, HD), 0)
-
-    def fill(at, i):
-        lanes = jnp.sum(jnp.where(diagonal, of_owner(logs, at, i), 0.0), axis=0, keepdims=True)
+    off_lane = lax.broadcasted_iota(jnp.int32, (block_rows, HD), 1) - lax.broadcasted_iota(
+        jnp.int32, (block_rows, HD), 0
+    )
+    diagonal = [off_lane == i * block_rows for i in range(2)]
+    place = lax.broadcasted_iota(jnp.int32, (send_o.shape[1] - 2 * block_rows, HD), 0)
+
+    log_rows = place.shape[0]
+    spans = [(0, block_rows + log_rows), (block_rows + log_rows, block_rows)]
+
+    def fill(at):
+        lanes = sum(
+            jnp.sum(jnp.where(diagonal[i], of_owner(logs, at, i), 0.0), axis=0, keepdims=True)
+            for i in range(2)
+        )
         high = lanes.astype(BF16).astype(F32)
         middle = (lanes - high).astype(BF16).astype(F32)
         low = lanes - high - middle
         terms = jnp.where(place == 0, high, jnp.where(place == 1, middle, low))
-        send_o[i, at] = jnp.concatenate([of_owner(means, at, i), terms], axis=0).astype(BF16)
+        send_o[at] = jnp.concatenate(
+            [of_owner(means, at, 0), terms, of_owner(means, at, 1)], axis=0
+        ).astype(BF16)
+
+    def mean_copy(k, i):
+        return pltpu.make_async_remote_copy(
+            src_ref=send_o.at[peer_t[k], pl.ds(*spans[i])],
+            dst_ref=recv_o.at[t, pl.ds(*spans[i])],
+            send_sem=o_send_sem.at[i * n_t + k],
+            recv_sem=o_recv_sem.at[i * n_t + k],
+            device_id=(g, peer_t[k]),
+            device_id_type=MESH,
+        )
 
     def along_tp(k, i, source, target, send_sem, recv_sem):
         return pltpu.make_async_remote_copy(
@@ -309,18 +328,13 @@
             device_id_type=MESH,
         )
 
-    for i in range(2):
-        for at in range(n_t):
-            fill(at, i)
+    for at in range(n_t):
+        fill(at)
     pl.semaphore_wait(barrier, n_g + n_t - 2)
-    row_copies = [
-        [along_tp(k, i, send_o, recv_o, o_send_sem, o_recv_sem) for k in far_first[:-1]]
-        for i in range(2)
-    ]
-    for i in range(2):
-        for copy in row_copies[i]:
-            copy.start()
-        recv_o[i, t] = send_o[i, t]
+    row_copies = [[mean_copy(k, i) for k in far_first[:-1]] for i in range(2)]
+    for copy in row_copies[0] + row_copies[1]:
+        copy.start()
+    recv_o[t] = send_o[t]
 
     for load in loads[4:8]:
         load.wait()
@@ -362,15 +376,16 @@
     def finish_context(i):
         logs = []
         for at in range(n_t):
-            terms = recv_o[i, at, block_rows:].astype(F32)
+            terms = recv_o[at, block_rows : block_rows + log_rows].astype(F32)
             lanes = terms[0:1] + terms[1:2] + terms[2:3]
-            logs.append(jnp.sum(jnp.where(diagonal, lanes, 0.0), axis=-1, keepdims=True))
+            logs.append(jnp.sum(jnp.where(diagonal[i], lanes, 0.0), axis=-1, keepdims=True))
         joint = functools.reduce(jnp.maximum, logs + fresh[i])
         total, accum = 0.0, 0.0
         for at in range(n_t):
             weight = jnp.exp(logs[at] - joint)
             total = total + weight
-            accum = accum + weight * recv_o[i, at, :block_rows].astype(F32)
+            held = recv_o[at, i * spans[1][0] : i * spans[1][0] + block_rows]
+            accum = accum + weight * held.astype(F32)
         for at in range(steps):
             weight = jnp.where(seen[at], jnp.exp(fresh[i][at] - joint), 0.0)
             total = total + weight
@@ -455,12 +470,14 @@
     gate_copies = [
         along_grp(k, send_g.at[peer_g[k]], recv_g, g_send_sem, g_recv_sem) for k in range(1, n_g)
     ]
+    held_columns = []
     for i in range(2):
-        columns = part_gate(i)
+        held_columns.append(part_gate(i))
         for k in range(1, n_g):
             in_part = functools.reduce(jnp.logical_or, [peer_g[k] == b for b in parts[i]])
             pl.when(in_part)(gate_copies[k - 1].start)
-        wide = jnp.concatenate(columns, axis=1)
+    for i in range(2):
+        wide = jnp.concatenate(held_columns[i], axis=1)
         for at, b in enumerate(parts[i]):
             x_flat[b] = wide[at * group_rows : (at + 1) * group_rows]
     recv_g[g] = send_g[g]
@@ -571,8 +588,8 @@
             pltpu.VMEM((n_g, rows * height, HD), F32),
             pltpu.VMEM((KVH, group_rows, HD), F32),
             pltpu.VMEM((KVH, group_rows, HD), F32),
-            pltpu.VMEM((2, n_t, rows * height + 16, HD), BF16),
-            pltpu.VMEM((2, n_t, rows * height + 16, HD), BF16),
+            pltpu.VMEM((n_t, 2 * rows * height + 16, HD), BF16),
+            pltpu.VMEM((n_t, 2 * rows * height + 16, HD), BF16),
             pltpu.VMEM((2, rows * height, HD), BF16),
             pltpu.VMEM((n_g, rows * height, HD), BF16),
             pltpu.VMEM((2, n_t * rows * height, HD), F32),
@@ -621,6 +638,7 @@
         and heads % n_g == 0
         and n_g % kv_heads == 0
         and steps * (heads // n_g) == 8
+        and rows % 2 == 0
         and rows * steps == 8
     )
     if even:

time: 29.7 us -> 29.6 us (level)
  no operation moved by 1% of the time
where the time goes in v1:
time: 29.6 us; the launch traced here: 29.5 us
  Pallas kernels  28.8 us (97%)
  local copies, waits for them, and re-layouts  0.63 us (2%)
    pallas_call x1, Pallas kernels, moved_activations(): pl.pallas_call(functools.partial(layer_kernel, n_g, n_t), out_shape=pltpu...  28.8 us
    unnamed x1, local copies, waits for them, and re-layouts  0.63 us

profile of v1, /device:TPU:0, one launch (start us, length us, event | category | flops | bytes accessed | tf_op | source)
XLA Modules:
  0.0 29.5 jit_solution(12171534646997427925)
XLA Ops:
  0.0 28.8 %shard_map.100 = bf16[4,2,4096]{2,1,0:T(2,128)(2,1)S(1)} custom-call(s32[4]{0:T(128)} %lengths_hbm.1, bf16[4,2,4096]{2,1,0:T(2,128)(2,1)} %q_hbm.1, bf16[4,2,512]{2,1,0:T(2,128)(2,1)} %nk_hbm.1, bf16[4,2,512]{2,1,0:T(2,128)(2,1)} %nv_hbm.1, bf16[4,2,4096]{2,1,0:T(2,128)(2,1)} %res_hbm.1, f32[32,128]{1,0:T(8,128)} %bitcast.5, bf16[4,128,512]{2,1,0:T(8,128)(2,1)} %ck_hbm.1, ...), custom_call_target="tpu_custom_call" | custom-call | tf_op jit(solution)/shard_map/pallas_call | solution.py:569
  28.8 0.6 %copy.12 = bf16[4,2,4096]{2,1,0:T(2,128)(2,1)} copy(bf16[4,2,4096]{2,1,0:T(2,128)(2,1)S(1)} %shard_map.100) | data formatting | bytes 131072

commit v2 on v1

--- a/solution.py
+++ b/solution.py
@@ -435,15 +435,13 @@
         x_spread.start(i)
 
     parts = [[blocks_of(at)[i] for at in range(n_t)] for i in range(2)]
-    part_rows = n_t * group_rows
+    all_rows = n_g * group_rows
     gains = [gain[pl.ds(g * per_col + c, 1)] for c in range(per_col)]
 
-    def part_gate(i):
-        x_spread.wait_recv(parts[i])
-        x_rows[i] = jnp.concatenate([recv_x[b].astype(F32) for b in parts[i]], axis=0)
-        columns = [
-            x_rows.at[i][pl.ds(c, part_rows, stride=per_col), :] for c in range(per_col)
-        ]
+    def part_gate():
+        x_spread.wait_recv(range(n_g))
+        x_rows[...] = recv_x[...].astype(F32).reshape(x_rows.shape)
+        columns = [x_rows[pl.ds(c, all_rows, stride=per_col), :] for c in range(per_col)]
         squares = jnp.sum(
             functools.reduce(jnp.add, [c * c for c in columns]), axis=-1, keepdims=True
         )
@@ -453,8 +451,8 @@
         )
         spare_lane = lax.broadcasted_iota(jnp.int32, gate.shape, 1) >= units
         gate = jnp.where(spare_lane, squares, gate)
-        for at, b in enumerate(parts[i]):
-            send_g[b] = gate[at * group_rows : (at + 1) * group_rows].astype(BF16)
+        for b in range(n_g):
+            send_g[b] = gate[b * group_rows : (b + 1) * group_rows].astype(BF16)
         return columns
 
     def along_grp(k, source, target, send_sem, recv_sem):
@@ -470,16 +468,10 @@
     gate_copies = [
         along_grp(k, send_g.at[peer_g[k]], recv_g, g_send_sem, g_recv_sem) for k in range(1, n_g)
     ]
-    held_columns = []
-    for i in range(2):
-        held_columns.append(part_gate(i))
-        for k in range(1, n_g):
-            in_part = functools.reduce(jnp.logical_or, [peer_g[k] == b for b in parts[i]])
-            pl.when(in_part)(gate_copies[k - 1].start)
-    for i in range(2):
-        wide = jnp.concatenate(held_columns[i], axis=1)
-        for at, b in enumerate(parts[i]):
-            x_flat[b] = wide[at * group_rows : (at + 1) * group_rows]
+    columns = part_gate()
+    for copy in gate_copies:
+        copy.start()
+    x_flat[...] = jnp.concatenate(columns, axis=1).reshape(x_flat.shape)
     recv_g[g] = send_g[g]
     loads[9].wait()
     wd[...] = jnp.concatenate([wd32[...], spare], axis=0).astype(BF16)
@@ -592,7 +584,7 @@
             pltpu.VMEM((n_t, 2 * rows * height + 16, HD), BF16),
             pltpu.VMEM((2, rows * height, HD), BF16),
             pltpu.VMEM((n_g, rows * height, HD), BF16),
-            pltpu.VMEM((2, n_t * rows * height, HD), F32),
+            pltpu.VMEM((n_g * rows * height, HD), F32),
             pltpu.VMEM((n_g, group_rows, depth), F32),
             pltpu.VMEM((n_g, group_rows, wide), BF16),
             pltpu.VMEM((n_g, group_rows, wide), BF16),

time: 29.6 us -> 29.7 us (level)
  no operation moved by 1% of the time
where the time goes in v2:
time: 29.7 us; the launch traced here: 29.6 us
  Pallas kernels  28.9 us (97%)
  local copies, waits for them, and re-layouts  0.63 us (2%)
    pallas_call x1, Pallas kernels, moved_activations(): pl.pallas_call(functools.partial(layer_kernel, n_g, n_t), out_shape=pltpu...  28.9 us
    unnamed x1, local copies, waits for them, and re-layouts  0.63 us

profile of v2, /device:TPU:0, one launch (start us, length us, event | category | flops | bytes accessed | tf_op | source)
XLA Modules:
  0.0 29.6 jit_solution(10067718153859900695)
XLA Ops:
  0.0 28.9 %shard_map.100 = bf16[4,2,4096]{2,1,0:T(2,128)(2,1)S(1)} custom-call(s32[4]{0:T(128)} %lengths_hbm.1, bf16[4,2,4096]{2,1,0:T(2,128)(2,1)} %q_hbm.1, bf16[4,2,512]{2,1,0:T(2,128)(2,1)} %nk_hbm.1, bf16[4,2,512]{2,1,0:T(2,128)(2,1)} %nv_hbm.1, bf16[4,2,4096]{2,1,0:T(2,128)(2,1)} %res_hbm.1, f32[32,128]{1,0:T(8,128)} %bitcast.5, bf16[4,128,512]{2,1,0:T(8,128)(2,1)} %ck_hbm.1, ...), custom_call_target="tpu_custom_call" | custom-call | tf_op jit(solution)/shard_map/pallas_call | solution.py:561
  28.9 0.6 %copy.12 = bf16[4,2,4096]{2,1,0:T(2,128)(2,1)} copy(bf16[4,2,4096]{2,1,0:T(2,128)(2,1)S(1)} %shard_map.100) | data formatting | bytes 131072

commit v3 on v2

--- a/solution.py
+++ b/solution.py
@@ -310,8 +310,8 @@
 
     def mean_copy(k, i):
         return pltpu.make_async_remote_copy(
-            src_ref=send_o.at[peer_t[k], pl.ds(*spans[i])],
-            dst_ref=recv_o.at[t, pl.ds(*spans[i])],
+            src_ref=send_o.at[peer_t[k]],
+            dst_ref=recv_o.at[t],
             send_sem=o_send_sem.at[i * n_t + k],
             recv_sem=o_recv_sem.at[i * n_t + k],
             device_id=(g, peer_t[k]),
@@ -331,7 +331,7 @@
     for at in range(n_t):
         fill(at)
     pl.semaphore_wait(barrier, n_g + n_t - 2)
-    row_copies = [[mean_copy(k, i) for k in far_first[:-1]] for i in range(2)]
+    row_copies = [[mean_copy(k, 0) for k in far_first[:-1]], []]
     for copy in row_copies[0] + row_copies[1]:
         copy.start()
     recv_o[t] = send_o[t]

time: 29.7 us -> 29.8 us (level)
  no operation moved by 1% of the time
where the time goes in v3:
time: 29.8 us; the launch traced here: 29.7 us
  Pallas kernels  29 us (97%)
  local copies, waits for them, and re-layouts  0.63 us (2%)
    pallas_call x1, Pallas kernels, moved_activations(): pl.pallas_call(functools.partial(layer_kernel, n_g, n_t), out_shape=pltpu...  29 us
    unnamed x1, local copies, waits for them, and re-layouts  0.63 us

profile of v3, /device:TPU:0, one launch (start us, length us, event | category | flops | bytes accessed | tf_op | source)
XLA Modules:
  0.0 29.7 jit_solution(9497985219830995896)
XLA Ops:
  0.0 29.0 %shard_map.100 = bf16[4,2,4096]{2,1,0:T(2,128)(2,1)S(1)} custom-call(s32[4]{0:T(128)} %lengths_hbm.1, bf16[4,2,4096]{2,1,0:T(2,128)(2,1)} %q_hbm.1, bf16[4,2,512]{2,1,0:T(2,128)(2,1)} %nk_hbm.1, bf16[4,2,512]{2,1,0:T(2,128)(2,1)} %nv_hbm.1, bf16[4,2,4096]{2,1,0:T(2,128)(2,1)} %res_hbm.1, f32[32,128]{1,0:T(8,128)} %bitcast.5, bf16[4,128,512]{2,1,0:T(8,128)(2,1)} %ck_hbm.1, ...), custom_call_target="tpu_custom_call" | custom-call | tf_op jit(solution)/shard_map/pallas_call | solution.py:561
  29.1 0.6 %copy.12 = bf16[4,2,4096]{2,1,0:T(2,128)(2,1)} copy(bf16[4,2,4096]{2,1,0:T(2,128)(2,1)S(1)} %shard_map.100) | data formatting | bytes 131072
